TPU v7x, 128 devices: a whole 4x4x4 slice. The times are simulated.
128 devices in a mesh: blk: 4 (over x_lo, core), dom: 32 (over z, y, x_hi).
Axes of the slice: x: 4 (x_hi: 2, x_lo: 2; x = x_hi * 2 + x_lo), y: 4, z: 4, core: 2. Of those that a mesh axis runs over, the one named last changes fastest.
Arguments:
- node_feats: bfloat16 [65536, 512], P(('blk', 'dom')), may hold values from -6 to 6
- send_rows: int32 [128, 32, 32], P(('blk', 'dom')), may hold values from 0 to 511
- neighbour_slots: int32 [65536, 8], P(('blk', 'dom')), may hold values from 0 to 1535
- slot_mask: int32 [65536, 8], P(('blk', 'dom')), may hold values 0 or 1
- gate_weight: bfloat16 [512, 512], replicated, may hold values from -0.25 to 0.25
- source_weight: bfloat16 [512, 1024], replicated, may hold values from -0.25 to 0.25
- qkv_weight: bfloat16 [512, 1536], replicated, may hold values from -0.26516504 to 0.26516504
- out_weight: bfloat16 [512, 512], replicated, may hold values from -0.25 to 0.25
- cotangent: bfloat16 [65536, 512], P(('blk', 'dom')), may hold values from -6 to 6
Outputs:
- layer_out: bfloat16 [65536, 512], P(('blk', 'dom'))
- feats_grad: bfloat16 [65536, 512], P(('blk', 'dom'))
- gate_grad: float32 [512, 512], replicated
- source_grad: float32 [512, 1024], replicated
- qkv_grad: float32 [512, 1536], replicated
- out_grad: float32 [512, 512], replicated
Inputs may be any that keep to these rules, and one draw needn't show every extreme that they name: `send_rows`: local node indices of the sending device. `neighbour_slots`: rows below 512 are the device's own nodes, the others received rows.
All inputs are finite; a program needn't handle non-finite values. No bound on the sum of `slot_mask` on one device may be relied on, other than what follows from the above.
Results may differ from a plain program's by a relative error of at most 0.035.
Values may be sent and summed in bfloat16 or wider, within the bound.
No kernel may reach another device: no remote copies, remote signals or barrier semaphores. Data moves between devices by JAX's collectives and lax.ppermute only.
A program may use at most 256 MiB of HBM per device.

v0:
```python
import math
import jax
import jax.numpy as jnp
from jax import lax
from jax.sharding import PartitionSpec as P

HEADS = 8
HDIM = 64


def body(
    node_feats,
    send_rows,
    neighbour_slots,
    slot_mask,
    gate_weight,
    source_weight,
    qkv_weight,
    out_weight,
    cotangent,
):
    node_count, feat_width = node_feats.shape
    head_count = HEADS
    head_width = HDIM
    score_scale = 1.0 / math.sqrt(HDIM)
    peer_count = lax.axis_size("dom")
    outgoing = node_feats[send_rows[0]]
    incoming = lax.all_to_all(outgoing, "dom", split_axis=0, concat_axis=0, tiled=True)
    table = jnp.concatenate([node_feats, incoming.reshape(-1, feat_width)], axis=0)
    table_rows = table.shape[0]
    gate_term = jnp.dot(node_feats, gate_weight, preferred_element_type=jnp.float32)
    source_terms = jnp.dot(table, source_weight, preferred_element_type=jnp.float32)
    edge_source = source_terms[neighbour_slots]
    gate_open = jax.nn.sigmoid(gate_term[:, None, :] + edge_source[:, :, :feat_width])
    edge_value = edge_source[:, :, feat_width:]
    mask_float = slot_mask.astype(jnp.float32)
    slot_weight = mask_float / jnp.maximum(jnp.sum(mask_float, axis=1, keepdims=True), 1.0)
    message = jnp.sum(slot_weight[:, :, None] * gate_open * edge_value, axis=1)
    qkv = jnp.dot(node_feats, qkv_weight, preferred_element_type=jnp.float32).astype(jnp.bfloat16)
    queries = qkv[:, :feat_width].reshape(node_count, head_count, head_width)
    keys_vals = lax.all_gather(qkv[:, feat_width:], "blk", axis=0, tiled=True)
    seq_len = keys_vals.shape[0]
    all_keys = keys_vals[:, :feat_width].reshape(seq_len, head_count, head_width)
    all_values = keys_vals[:, feat_width:].reshape(seq_len, head_count, head_width)
    scores = (
        jnp.einsum("ihe,jhe->hij", queries, all_keys, preferred_element_type=jnp.float32)
        * score_scale
    )
    row_top = jnp.max(scores, axis=2, keepdims=True)
    raw_weights = jnp.exp(scores - row_top)
    row_total = jnp.sum(raw_weights, axis=2, keepdims=True)
    prob_weights = raw_weights / row_total
    prob_half = prob_weights.astype(jnp.bfloat16)
    mixed = (
        jnp.einsum("hij,jhe->ihe", prob_half, all_values, preferred_element_type=jnp.float32)
        .astype(jnp.bfloat16)
        .reshape(node_count, feat_width)
    )
    attended = jnp.dot(mixed, out_weight, preferred_element_type=jnp.float32)
    layer_out = (node_feats.astype(jnp.float32) + message + attended).astype(jnp.bfloat16)
    upstream = cotangent.astype(jnp.float32)
    grad_out_w = jnp.einsum("nd,ne->de", mixed, cotangent, preferred_element_type=jnp.float32)
    d_mixed = jnp.einsum(
        "ne,de->nd", cotangent, out_weight, preferred_element_type=jnp.float32
    ).astype(jnp.bfloat16)
    d_heads = d_mixed.reshape(node_count, head_count, head_width)
    row_delta = jnp.sum(
        d_heads.astype(jnp.float32)
        * mixed.reshape(node_count, head_count, head_width).astype(jnp.float32),
        axis=2,
    )
    d_probs = jnp.einsum("ihe,jhe->hij", d_heads, all_values, preferred_element_type=jnp.float32)
    d_scores = (prob_weights * (d_probs - row_delta.T[:, :, None]) * score_scale).astype(
        jnp.bfloat16
    )
    d_query = jnp.einsum(
        "hij,jhe->ihe", d_scores, all_keys, preferred_element_type=jnp.float32
    ).reshape(node_count, feat_width)
    count = node_count * lax.axis_size("blk")
    d_key = jnp.einsum("hij,ihe->jhe", d_scores, queries, preferred_element_type=jnp.float32)
    d_value = jnp.einsum("hij,ihe->jhe", prob_half, d_heads, preferred_element_type=jnp.float32)
    d_keyval = lax.psum_scatter(
        jnp.concatenate(
            [d_key.reshape(count, feat_width), d_value.reshape(count, feat_width)], axis=1
        ),
        "blk",
        scatter_dimension=0,
        tiled=True,
    )
    d_qkv = jnp.concatenate([d_query, d_keyval], axis=1).astype(jnp.bfloat16)
    grad_qkv_w = jnp.einsum("nd,nf->df", node_feats, d_qkv, preferred_element_type=jnp.float32)
    d_attn_input = jnp.einsum("nf,df->nd", d_qkv, qkv_weight, preferred_element_type=jnp.float32)
    edge_up = slot_weight[:, :, None] * upstream[:, None, :]
    d_edge_value = edge_up * gate_open
    d_edge_logit = edge_up * edge_value * gate_open * (1.0 - gate_open)
    d_gate = jnp.sum(d_edge_logit, axis=1).astype(jnp.bfloat16)
    edge_terms = jnp.concatenate([d_edge_logit, d_edge_value], axis=2).reshape(-1, 2 * feat_width)
    d_source = jax.ops.segment_sum(
        edge_terms, neighbour_slots.reshape(-1), num_segments=table_rows
    ).astype(jnp.bfloat16)
    grad_source_w = jnp.einsum("td,tf->df", table, d_source, preferred_element_type=jnp.float32)
    grad_gate_w = jnp.einsum("nd,nf->df", node_feats, d_gate, preferred_element_type=jnp.float32)
    d_table = jnp.einsum("tf,df->td", d_source, source_weight, preferred_element_type=jnp.float32)
    returned = lax.all_to_all(
        d_table[node_count:].reshape(peer_count, -1, feat_width).astype(jnp.bfloat16),
        "dom",
        split_axis=0,
        concat_axis=0,
        tiled=True,
    ).astype(jnp.float32)
    d_sent = jax.ops.segment_sum(
        returned.reshape(-1, feat_width), send_rows[0].reshape(-1), num_segments=node_count
    )
    d_gate_input = jnp.einsum("nf,df->nd", d_gate, gate_weight, preferred_element_type=jnp.float32)
    feats_grad = (upstream + d_attn_input + d_table[:node_count] + d_gate_input + d_sent).astype(
        jnp.bfloat16
    )
    weight_sums = lax.psum((grad_gate_w, grad_source_w, grad_qkv_w, grad_out_w), ("blk", "dom"))
    return (layer_out, feats_grad, weight_sums[0], weight_sums[1], weight_sums[2], weight_sums[3])


def solution(mesh):
    return jax.shard_map(
        body,
        mesh=mesh,
        in_specs=(
            P(("blk", "dom"), None),
            P(("blk", "dom"), None, None),
            P(("blk", "dom"), None),
            P(("blk", "dom"), None),
            P(),
            P(),
            P(),
            P(),
            P(("blk", "dom"), None),
        ),
        out_specs=(P(("blk", "dom"), None), P(("blk", "dom"), None), P(), P(), P(), P()),
        check_vma=False,
    )
```

profile of v0, /device:TPU:1, one launch (start us, length us, event | category | flops | bytes accessed | tf_op | source)
XLA Modules:
  0.0 508.1 jit_solution(13844792690348114465)
XLA Ops:
  7.2 0.0 all-gather.2.cloned.1.call-start
  7.2 1.3 copy-done
  8.6 2.0 convolution_convert_fusion
  10.6 1.1 copy-done.9
  11.8 1.1 slice.39
  12.8 0.0 all-gather.2.cloned.1.call-update
  12.9 0.0 reduce-scatter.2.cloned.1.call-start
  12.9 1.1 slice.41
  14.0 1.0 copy.27
  15.0 0.5 convolution_convert_fusion.1
  15.5 47.7 %all-gather.2.cloned.1.call-done = bf16[2048,1024]{1,0:T(8,128)(2,1)} async-done(((bf16[512,1024]{1,0:T(8,128)(2,1)}), bf16[2048,1024]{1,0:T(8,128)(2,1)}) %all-gather.2.cloned.1.call-update) | async-done | bytes 4194320 | tf_op jit(solution)/shard_map/all_gather | solution.py:41
  63.2 4.5 fusion.36
  67.7 4.0 copy.28
  71.7 3.9 copy.26
  75.6 16.6 %fusion.37 = (f32[8,512]{1,0:T(8,128)S(1)}, f32[8,512,2048]{2,1,0:T(8,128)}) fusion(bf16[512,8,64]{0,2,1:T(8,128)(2,1)S(1)} %bitcast.82, bf16[2048,8,64]{0,2,1:T(8,128)(2,1)} %bitcast.71), kind=kOutput, calls=%fused_computation.67 | convolution fusion | flops 1098909696 | bytes 36192256 | tf_op jit(solution)/shard_map/sub | solution.py:50
  92.2 19.0 %fusion.8 = bf16[8,512,2048]{2,1,0:T(8,128)(2,1)} fusion(f32[8,512,2048]{2,1,0:T(8,128)} %get-tuple-element.29, f32[8,512]{1,0:T(8,128)S(1)} %get-tuple-element.28), kind=kLoop, calls=%fused_computation.15 | loop fusion | flops 16777216 | bytes 50348032 | tf_op jit(solution)/shard_map/convert_element_type | solution.py:53
  111.3 13.0 %multiply_reduce_fusion.2 = (f32[512,8]{0,1:T(8,128)}, bf16[8,64,512]{2,1,0:T(8,128)(2,1)}) fusion(bf16[512,512]{0,1:T(8,128)(2,1)S(1)} %convolution_convert_fusion.1, bf16[2048,8,64]{0,2,1:T(8,128)(2,1)} %bitcast.73, bf16[8,512,2048]{2,1,0:T(8,128)(2,1)} %fusion.8), kind=kOutput, calls=%fused_computation.49 | convolution fusion | flops 1075048448 | bytes 19939328 | tf_op jit(solution)/shard_map/hij,jhe->ihe/dot_general | solution.py:55
  124.3 10.8 %fusion.40 = f32[8,64,2048]{2,1,0:T(8,128)} fusion(bf16[512,8,64]{0,2,1:T(8,128)(2,1)S(1)} %bitcast.77, bf16[8,512,2048]{2,1,0:T(8,128)(2,1)} %fusion.8), kind=kOutput, calls=%fused_computation.70 | convolution fusion | flops 1073741824 | bytes 21495808 | tf_op jit(solution)/shard_map/hij,ihe->jhe/dot_general | solution.py:81
  135.1 13.4 %multiply_convert_fusion = bf16[8,512,2048]{2,1,0:T(8,128)(2,1)S(1)} fusion(bf16[512,8,64]{0,2,1:T(8,128)(2,1)S(1)} %bitcast.78, bf16[2048,8,64]{0,2,1:T(8,128)(2,1)} %bitcast.74, f32[8,512]{1,0:T(8,128)} %bitcast.85, f32[8,512,2048]{2,1,0:T(8,128)} %get-tuple-element.29, f32[8,512]{1,0:T(8,128)S(1)} %get-tuple-element.28), kind=kOutput, calls=%fused_computation.5 | convolution fusion | flops 1115684864 | bytes 52985856 | tf_op jit(solution)/shard_map/ihe,jhe->hij/dot_general | solution.py:72
  148.5 7.0 %fusion.39 = f32[8,64,2048]{2,1,0:T(8,128)} fusion(bf16[512,8,64]{0,2,1:T(8,128)(2,1)} %bitcast.81, bf16[8,512,2048]{2,1,0:T(8,128)(2,1)S(1)} %multiply_convert_fusion), kind=kOutput, calls=%fused_computation.69 | convolution fusion | flops 1073741824 | bytes 21495808 | tf_op jit(solution)/shard_map/hij,ihe->jhe/dot_general | solution.py:80
  155.5 0.0 copy-done.2
  155.5 7.8 %pad_maximum_fusion = f32[2048,1024]{0,1:T(8,128)} fusion(f32[2048,512]{0,1:T(8,128)} %bitcast.69, f32[2048,512]{0,1:T(8,128)} %bitcast.70), kind=kLoop, calls=%fused_computation.25 | loop fusion | flops 2097152 | bytes 16777216 | tf_op jit(solution)/shard_map/concatenate | solution.py:83
  163.3 0.7 copy-done.14
  164.0 0.1 reshape.105
  164.1 0.3 copy-done.1
  164.3 5.1 gather_fusion
  169.4 9.2 %all-to-all-start = ((bf16[32,32,512]{2,1,0:T(8,128)(2,1)}), bf16[32,32,512]{2,1,0:T(8,128)(2,1)}, u32[]{:S(2)}, u32[]{:S(2)}) async-start(bf16[32,32,512]{2,1,0:T(8,128)(2,1)} %bitcast.79), calls=%async_computation | async-start | bytes 2097152 | tf_op jit(solution)/shard_map/all_to_all | solution.py:28
  178.7 0.2 all-reduce.3.cloned.1.call-start
  178.9 1.1 convert_element_type.58
  180.0 0.8 copy.29
  180.8 0.1 copy.25
  181.0 0.2 reshape.113
  181.2 0.1 copy.24
  181.3 1.1 reshape.121
  182.4 1.4 fusion.38
  183.8 25.8 %all-to-all-done = bf16[32,32,512]{2,1,0:T(8,128)(2,1)} async-done(((bf16[32,32,512]{2,1,0:T(8,128)(2,1)}), bf16[32,32,512]{2,1,0:T(8,128)(2,1)}, u32[]{:S(2)}, u32[]{:S(2)}) %all-to-all-start) | async-done | bytes 1048608 | tf_op jit(solution)/shard_map/all_to_all | solution.py:28
  209.6 6.0 %fusion.26 = f32[1536,1024]{1,0:T(8,128)} fusion(bf16[512,1024]{1,0:T(8,128)(2,1)} %param.14, bf16[1024,512]{1,0:T(8,128)(2,1)} %bitcast.2, bf16[512,512]{1,0:T(8,128)(2,1)S(1)} %copy-done.1), kind=kOutput, calls=%fused_computation.50 | convolution fusion | flops 1613758464 | bytes 8912896 | tf_op jit(solution)/shard_map/dot_general | solution.py:32
  215.6 25.1 %gather_fusion.1 = f32[4096,1024]{1,0:T(8,128)} fusion(f32[1536,1024]{1,0:T(8,128)} %fusion.26, s32[4096]{0:T(1024)S(1)} %broadcast_clamp_fusion), kind=kCustom, calls=%fused_computation.1 | custom fusion | bytes 33570816 | tf_op jit(solution)/shard_map/gather | solution.py:33
  240.7 18.9 %fusion.34 = (bf16[512,512]{1,0:T(8,128)(2,1)S(1)}, f32[512,8,512]{2,1,0:T(8,128)}, f32[512,8,512]{2,1,0:T(8,128)}, f32[512,512]{1,0:T(8,128)}) fusion(f32[512,8,1024]{2,1,0:T(8,128)} %bitcast.68, f32[512,512]{1,0:T(8,128)} %fusion.38, f32[512,512]{1,0:T(8,128)} %convert_element_type.58, f32[512,8]{1,0:T(8,128)S(1)} %copy.24), kind=kLoop, calls=%fused_computation.65 | loop fusion | flops 28835840 | bytes 37240832 | tf_op jit(solution)/shard_map/reduce_sum | solution.py:96
  259.6 38.4 %scatter_custom_fusion = f32[1536,1024]{1,0:T(8,128)} fusion(s32[4096]{0:T(1024)S(1)} %reshape.121, f32[512,8,512]{2,1,0:T(8,128)} %get-tuple-element.24, f32[]{:T(128)} %constant.2.clone.1, f32[512,8,512]{2,1,0:T(8,128)} %get-tuple-element.23, f32[]{:T(128)} %constant.7.clone.1), kind=kCustom, calls=%fused_computation.10 | custom fusion | flops 8388608 | bytes 23068680 | tf_op jit(solution)/shard_map/scatter-add | solution.py:98
  298.1 1.4 convolution_bitcast_fusion.1
  299.5 6.2 %fusion.20 = f32[512,1024]{1,0:T(8,128)} fusion(f32[1536,1024]{1,0:T(8,128)} %scatter_custom_fusion, bf16[1024,512]{1,0:T(8,128)(2,1)} %bitcast.2, bf16[512,512]{1,0:T(8,128)(2,1)S(1)} %copy-done.1), kind=kOutput, calls=%fused_computation.36 | convolution fusion | flops 1615331328 | bytes 9961472 | tf_op jit(solution)/shard_map/td,tf->df/dot_general | solution.py:101
  305.8 1.4 fusion.41
  307.2 12.4 %convolution_convert_fusion.2 = bf16[8,64,512]{2,1,0:T(8,128)(2,1)} fusion(bf16[2048,8,64]{0,2,1:T(8,128)(2,1)} %bitcast.72, bf16[8,512,2048]{2,1,0:T(8,128)(2,1)} %copy-done.2), kind=kOutput, calls=%fused_computation.47 | convolution fusion | flops 1074003968 | bytes 19398656 | tf_op jit(solution)/shard_map/hij,jhe->ihe/dot_general | solution.py:76
  319.6 1.7 convert.13
  321.4 1.0 copy-done.10
  322.3 3.7 convolution_bitcast_fusion
  326.0 0.0 all-reduce.3.cloned.1.call-update
  326.0 4.9 fusion.22
  331.0 1.7 copy-done.12
  332.6 1.1 slice.64
  333.8 4.9 all-to-all-start.1
  338.7 0.1 reshape.129
  338.8 2.9 fusion.25
  341.7 2.8 fusion.24
  344.5 1.4 convolution_add_fusion
  346.0 13.1 %all-to-all-done.1 = bf16[32,32,512]{2,1,0:T(8,128)(2,1)} async-done(((bf16[32,32,512]{2,1,0:T(8,128)(2,1)}), bf16[32,32,512]{2,1,0:T(8,128)(2,1)}, u32[]{:S(2)}, u32[]{:S(2)}) %all-to-all-start.1) | async-done | bytes 1048608 | tf_op jit(solution)/shard_map/all_to_all | solution.py:104
  359.0 9.4 %scatter_custom_fusion.1 = f32[512,512]{1,0:T(8,128)} fusion(f32[512,512]{1,0:T(8,128)} %convolution_add_fusion, s32[1024]{0:T(1024)S(1)} %reshape.129, bf16[1024,512]{1,0:T(8,128)(2,1)} %bitcast.26), kind=kCustom, calls=%fused_computation.32 | custom fusion | flops 1048576 | bytes 2097152 | tf_op jit(solution)/shard_map/scatter-add | solution.py:111
  368.4 2.1 convert_element_type.66
  370.6 120.5 %all-reduce.3.cloned.1.call-done = (f32[512,512]{0,1:T(8,128)}, f32[512,1024]{1,0:T(8,128)}, f32[512,1536]{0,1:T(8,128)}, f32[512,512]{1,0:T(8,128)}) async-done(((f32[512,512]{0,1:T(8,128)}, f32[512,1024]{1,0:T(8,128)}, f32[512,1536]{0,1:T(8,128)}, f32[512,512]{1,0:T(8,128)}), (f32[512,512]{0,1:T(8,128)}, f32[512,1024]{1,0:T(8,128)}, f32[512,1536]{0,1:T(8,128)}, ...) | async-done | bytes 7340048 | tf_op jit(solution)/shard_map/psum | solution.py:118
  491.0 2.6 copy.30
  493.6 3.5 copy.31
  497.2 3.2 copy.37
  500.3 1.0 copy.38
  (34 shorter events, 0.1 us)
Async XLA Ops:
  7.2 1.4 copy-start
  7.2 7.8 %copy-start.3 = (bf16[512,512]{1,0:T(8,128)(2,1)S(1)}, bf16[512,512]{1,0:T(8,128)(2,1)}, u32[]{:S(2)}) copy-start(bf16[512,512]{1,0:T(8,128)(2,1)} %param.17) | copy-start | bytes 1572868
  7.2 7.8 %copy-start.5 = (bf16[512,512]{1,0:T(8,128)(2,1)S(1)}, bf16[512,512]{1,0:T(8,128)(2,1)}, u32[]{:S(2)}) copy-start(bf16[512,512]{1,0:T(8,128)(2,1)} %param.16) | copy-start | bytes 1572868
  7.2 56.0 %all-gather.2.cloned.1.call-start = ((), (), s32[]{:S(2)}) async-start(), calls=%async_computation.3 | async-start | bytes 5242880 | tf_op jit(solution)/shard_map/all_gather | solution.py:41
  10.6 1.1 copy-start.9
  12.9 306.7 %reduce-scatter.2.cloned.1.call-start = ((), (), s32[]{:S(2)}) async-start(), calls=%async_computation.4 | async-start | bytes 10485760 | tf_op jit(solution)/shard_map/reduce_scatter | solution.py:82
  67.7 7.9 %copy-start.8 = (bf16[512,512]{0,1:T(8,128)(2,1)S(1)}, bf16[512,512]{0,1:T(8,128)(2,1)}, u32[]{:S(2)}) copy-start(bf16[512,512]{0,1:T(8,128)(2,1)} %copy.27) | copy-start | bytes 1572868
  148.5 7.0 %copy-start.2 = (bf16[8,512,2048]{2,1,0:T(8,128)(2,1)}, bf16[8,512,2048]{2,1,0:T(8,128)(2,1)S(1)}, u32[]{:S(2)}) copy-start(bf16[8,512,2048]{2,1,0:T(8,128)(2,1)S(1)} %multiply_convert_fusion) | copy-start | bytes 50331652
  163.3 0.7 copy-start.14
  163.3 1.1 copy-start.1
  164.3 15.7 %copy-start.13 = (s32[512,8]{0,1:T(8,128)S(1)}, s32[512,8]{0,1:T(8,128)}, u32[]{:S(2)}) copy-start(s32[512,8]{0,1:T(8,128)} %param.11) | copy-start | bytes 49156
  164.3 16.8 %copy-start.15 = (s32[512,8]{0,1:T(8,128)S(1)}, s32[512,8]{0,1:T(8,128)}, u32[]{:S(2)}) copy-start(s32[512,8]{0,1:T(8,128)} %param.12) | copy-start | bytes 49156
  164.3 18.1 %copy-start.6 = (bf16[512,512]{1,0:T(8,128)(2,1)S(1)}, bf16[512,512]{1,0:T(8,128)(2,1)}, u32[]{:S(2)}) copy-start(bf16[512,512]{1,0:T(8,128)(2,1)} %param.13) | copy-start | bytes 1572868
  169.4 40.2 %all-to-all-start = ((bf16[32,32,512]{2,1,0:T(8,128)(2,1)}), bf16[32,32,512]{2,1,0:T(8,128)(2,1)}, u32[]{:S(2)}, u32[]{:S(2)}) async-start(bf16[32,32,512]{2,1,0:T(8,128)(2,1)} %bitcast.79), calls=%async_computation | async-start | bytes 2097152 | tf_op jit(solution)/shard_map/all_to_all | solution.py:28
  178.7 312.4 %all-reduce.3.cloned.1.call-start = ((), (), s32[]{:S(2)}) async-start(), calls=%async_computation.5 | async-start | bytes 14680064 | tf_op jit(solution)/shard_map/psum | solution.py:118
  298.1 7.7 %copy-start.4 = (bf16[8,64,512]{2,1,0:T(8,128)(2,1)S(1)}, bf16[8,64,512]{2,1,0:T(8,128)(2,1)}, u32[]{:S(2)}) copy-start(bf16[8,64,512]{2,1,0:T(8,128)(2,1)} %get-tuple-element.31) | copy-start | bytes 1572868
  321.3 1.0 copy-start.10
  331.0 1.7 copy-start.12
  333.8 25.3 %all-to-all-start.1 = ((bf16[32,32,512]{2,1,0:T(8,128)(2,1)}), bf16[32,32,512]{2,1,0:T(8,128)(2,1)}, u32[]{:S(2)}, u32[]{:S(2)}) async-start(bf16[32,32,512]{2,1,0:T(8,128)(2,1)} %bitcast.80), calls=%async_computation.2 | async-start | bytes 2097152 | tf_op jit(solution)/shard_map/all_to_all | solution.py:104
  338.8 5.7 %copy-start.7 = (bf16[512,512]{1,0:T(8,128)(2,1)S(1)}, bf16[512,512]{1,0:T(8,128)(2,1)}, u32[]{:S(2)}) copy-start(bf16[512,512]{1,0:T(8,128)(2,1)} %param.13) | copy-start | bytes 1572868
  491.0 9.3 %copy-start.11 = (f32[512,512]{1,0:T(8,128)S(1)}, f32[512,512]{1,0:T(8,128)}, u32[]{:S(2)}) copy-start(f32[512,512]{1,0:T(8,128)} %get-tuple-element.37) | copy-start | bytes 3145732
Sparse Core Ops, SparseCore 0:
  13.0 50.1 all-gather.1
  163.4 90.9 reduce-scatter.1
  326.2 164.8 all-reduce.2
where the time goes:
time: 515 us; the launch traced here: 508 us
  waiting for transfers between devices  207 us (40%)
  matrix products  108 us (21%)
  other arithmetic  98.5 us (19%)
  local copies, waits for them, and re-layouts  65.8 us (13%)
  starting transfers between devices  14.4 us (3%)
  between operations  14.2 us (3%)
    psum x1, waiting for transfers between devices, body(): lax.psum((grad_gate_w, grad_source_w, grad_qkv_w, grad_out_w), ('blk', 'd...  120 us
    all_gather x1, waiting for transfers between devices, body(): keys_vals = lax.all_gather(qkv[:, feat_width:], 'blk', axis=0, tiled=True)  47.7 us
    scatter-add x1, other arithmetic, body(): jax.ops.segment_sum(edge_terms, neighbour_slots.reshape(-1), num_segments...  38.4 us
    all_to_all x1, waiting for transfers between devices, body(): lax.all_to_all(outgoing, 'dom', split_axis=0, concat_axis=0, tiled=True)  25.8 us
    gather x1, local copies, waits for them, and re-layouts, body(): edge_source = source_terms[neighbour_slots]  25.1 us
    convert_element_type x1, other arithmetic, body(): prob_half = prob_weights.astype(jnp.bfloat16)  19 us
    reduce_sum x1, other arithmetic, body(): d_gate = jnp.sum(d_edge_logit, axis=1).astype(jnp.bfloat16)  18.9 us
    unnamed x37, local copies, waits for them, and re-layouts  17.2 us
  transfers between devices with their start and end apart: 5, of which 4 were waited for; matrix products, arithmetic and copies ran while one was open for 29% of the time, Pallas kernels for 0%

commit v1 on v0

--- a/solution.py
+++ b/solution.py
@@ -3,6 +3,7 @@
 import jax.numpy as jnp
 from jax import lax
 from jax.sharding import PartitionSpec as P
+from jax.lax import all_to_all, axis_size
 
 HEADS = 8
 HDIM = 64
@@ -38,7 +39,16 @@
     message = jnp.sum(slot_weight[:, :, None] * gate_open * edge_value, axis=1)
     qkv = jnp.dot(node_feats, qkv_weight, preferred_element_type=jnp.float32).astype(jnp.bfloat16)
     queries = qkv[:, :feat_width].reshape(node_count, head_count, head_width)
-    keys_vals = lax.all_gather(qkv[:, feat_width:], "blk", axis=0, tiled=True)
+    piece_in = qkv[:, feat_width:]
+    keys_vals = jnp.concatenate(
+        all_to_all(
+            jnp.stack([piece_in for _ in range(axis_size("blk"))]),
+            axis_name="blk",
+            split_axis=0,
+            concat_axis=0,
+        ),
+        axis=0,
+    )
     seq_len = keys_vals.shape[0]
     all_keys = keys_vals[:, :feat_width].reshape(seq_len, head_count, head_width)
     all_values = keys_vals[:, feat_width:].reshape(seq_len, head_count, head_width)

time: 515 us -> 532 us (1.033)
  local copies, waits for them, and re-layouts: 65.8 us -> 75.2 us
  starting transfers between devices: 14.4 us -> 22.2 us
    all_gather x1 -> x0, waiting for transfers between devices: 47.7 us -> none  [body(): keys_vals = lax.all_gather(qkv[:, feat_width:], 'blk', axis=0, tiled=True)]
    all_to_all x0 -> x1, waiting for transfers between devices: none -> 45.9 us  [body(): all_to_all(jnp.stack([piece_in for _ in range(axis_size('blk'))]), axis_n...]
    all_to_all x0 -> x1, starting transfers between devices: none -> 6.35 us  [body(): all_to_all(jnp.stack([piece_in for _ in range(axis_size('blk'))]), axis_n...]
    all_to_all x0 -> x1, local copies, waits for them, and re-layouts: none -> 6.3 us  [body(): all_to_all(jnp.stack([piece_in for _ in range(axis_size('blk'))]), axis_n...]
  transfers between devices with their start and end apart: 5 -> 5, of which waited for: 4 -> 4; matrix products, arithmetic and copies ran while one was open for 29% -> 28% of each run, Pallas kernels for 0% -> 0%
where the time goes in v1:
time: 532 us; the launch traced here: 525 us
  waiting for transfers between devices  206 us (39%)
  matrix products  108 us (20%)
  other arithmetic  98.6 us (19%)
  local copies, waits for them, and re-layouts  75.2 us (14%)
  starting transfers between devices  22.2 us (4%)
  between operations  14.5 us (3%)
    psum x1, waiting for transfers between devices, body(): lax.psum((grad_gate_w, grad_source_w, grad_qkv_w, grad_out_w), ('blk', 'd...  122 us
    all_to_all x1, waiting for transfers between devices, body(): all_to_all(jnp.stack([piece_in for _ in range(axis_size('blk'))]), axis_n...  45.9 us
    scatter-add x1, other arithmetic, body(): jax.ops.segment_sum(edge_terms, neighbour_slots.reshape(-1), num_segments...  38.4 us
    gather x1, local copies, waits for them, and re-layouts, body(): edge_source = source_terms[neighbour_slots]  25.4 us
    all_to_all x1, waiting for transfers between devices, body(): lax.all_to_all(outgoing, 'dom', split_axis=0, concat_axis=0, tiled=True)  25.1 us
    convert_element_type x1, other arithmetic, body(): prob_half = prob_weights.astype(jnp.bfloat16)  19 us
    reduce_sum x1, other arithmetic, body(): d_gate = jnp.sum(d_edge_logit, axis=1).astype(jnp.bfloat16)  19 us
    unnamed x37, local copies, waits for them, and re-layouts  17.3 us
  transfers between devices with their start and end apart: 5, of which 4 were waited for; matrix products, arithmetic and copies ran while one was open for 28% of the time, Pallas kernels for 0%

profile of v1, /device:TPU:1, one launch (start us, length us, event | category | flops | bytes accessed | tf_op | source)
XLA Modules:
  0.0 524.7 jit_solution(7222098018229012060)
XLA Ops:
  7.2 1.4 copy-done
  8.6 2.0 convolution_convert_fusion
  10.6 1.1 copy-done.6
  11.8 1.1 slice.39
  12.8 1.5 copy.37
  14.4 2.3 stack.2
  16.7 6.3 %all-to-all-start.1 = ((bf16[4,512,1024]{1,2,0:T(8,128)(2,1)}), bf16[4,512,1024]{1,2,0:T(8,128)(2,1)}, u32[]{:S(2)}, u32[]{:S(2)}) async-start(bf16[4,512,1024]{1,2,0:T(8,128)(2,1)} %stack.2), calls=%async_computation.1 | async-start | bytes 8388608 | tf_op jit(solution)/shard_map/all_to_all | solution.py:44
  23.0 1.0 copy.40
  24.0 0.5 convolution_convert_fusion.1
  24.5 45.9 %all-to-all-done.1 = bf16[4,512,1024]{1,2,0:T(8,128)(2,1)} async-done(((bf16[4,512,1024]{1,2,0:T(8,128)(2,1)}), bf16[4,512,1024]{1,2,0:T(8,128)(2,1)}, u32[]{:S(2)}, u32[]{:S(2)}) %all-to-all-start.1) | async-done | bytes 4194336 | tf_op jit(solution)/shard_map/all_to_all | solution.py:44
  70.4 6.3 %copy.38 = bf16[4,512,1024]{2,1,0:T(8,128)(2,1)} copy(bf16[4,512,1024]{1,2,0:T(8,128)(2,1)} %all-to-all-done.1) | data formatting | bytes 8388608 | tf_op jit(solution)/shard_map/all_to_all | solution.py:44
  76.7 4.5 fusion.36
  81.2 4.0 copy.41
  85.3 3.9 copy.39
  89.2 16.6 %fusion.37 = (f32[8,512]{1,0:T(8,128)S(1)}, f32[8,512,2048]{2,1,0:T(8,128)}) fusion(bf16[512,8,64]{0,2,1:T(8,128)(2,1)S(1)} %bitcast.84, bf16[2048,8,64]{0,2,1:T(8,128)(2,1)} %bitcast.73), kind=kOutput, calls=%fused_computation.67 | convolution fusion | flops 1098909696 | bytes 36192256 | tf_op jit(solution)/shard_map/sub | solution.py:60
  105.8 19.0 %fusion.8 = bf16[8,512,2048]{2,1,0:T(8,128)(2,1)} fusion(f32[8,512,2048]{2,1,0:T(8,128)} %get-tuple-element.41, f32[8,512]{1,0:T(8,128)S(1)} %get-tuple-element.40), kind=kLoop, calls=%fused_computation.15 | loop fusion | flops 16777216 | bytes 50348032 | tf_op jit(solution)/shard_map/convert_element_type | solution.py:63
  124.9 13.0 %multiply_reduce_fusion.2 = (f32[512,8]{0,1:T(8,128)}, bf16[8,64,512]{2,1,0:T(8,128)(2,1)}) fusion(bf16[512,512]{0,1:T(8,128)(2,1)S(1)} %convolution_convert_fusion.1, bf16[2048,8,64]{0,2,1:T(8,128)(2,1)} %bitcast.75, bf16[8,512,2048]{2,1,0:T(8,128)(2,1)} %fusion.8), kind=kOutput, calls=%fused_computation.49 | convolution fusion | flops 1075048448 | bytes 19939328 | tf_op jit(solution)/shard_map/hij,jhe->ihe/dot_general | solution.py:65
  137.9 10.8 %fusion.40 = f32[8,64,2048]{2,1,0:T(8,128)} fusion(bf16[512,8,64]{0,2,1:T(8,128)(2,1)S(1)} %bitcast.79, bf16[8,512,2048]{2,1,0:T(8,128)(2,1)} %fusion.8), kind=kOutput, calls=%fused_computation.70 | convolution fusion | flops 1073741824 | bytes 21495808 | tf_op jit(solution)/shard_map/hij,ihe->jhe/dot_general | solution.py:91
  148.7 13.4 %multiply_convert_fusion = bf16[8,512,2048]{2,1,0:T(8,128)(2,1)S(1)} fusion(bf16[512,8,64]{0,2,1:T(8,128)(2,1)S(1)} %bitcast.80, bf16[2048,8,64]{0,2,1:T(8,128)(2,1)} %bitcast.76, f32[8,512]{1,0:T(8,128)} %bitcast.87, f32[8,512,2048]{2,1,0:T(8,128)} %get-tuple-element.41, f32[8,512]{1,0:T(8,128)S(1)} %get-tuple-element.40), kind=kOutput, calls=%fused_computation.5 | convolution fusion | flops 1115684864 | bytes 52985856 | tf_op jit(solution)/shard_map/ihe,jhe->hij/dot_general | solution.py:82
  162.1 7.0 %fusion.39 = f32[8,64,2048]{2,1,0:T(8,128)} fusion(bf16[512,8,64]{0,2,1:T(8,128)(2,1)} %bitcast.83, bf16[8,512,2048]{2,1,0:T(8,128)(2,1)S(1)} %multiply_convert_fusion), kind=kOutput, calls=%fused_computation.69 | convolution fusion | flops 1073741824 | bytes 21495808 | tf_op jit(solution)/shard_map/hij,ihe->jhe/dot_general | solution.py:90
  169.1 0.0 copy-done.2
  169.1 7.8 %pad_maximum_fusion = f32[2048,1024]{0,1:T(8,128)} fusion(f32[2048,512]{0,1:T(8,128)} %bitcast.71, f32[2048,512]{0,1:T(8,128)} %bitcast.72), kind=kLoop, calls=%fused_computation.25 | loop fusion | flops 2097152 | bytes 16777216 | tf_op jit(solution)/shard_map/concatenate | solution.py:93
  176.9 0.0 reduce-scatter.2.cloned.1.call-update
  176.9 0.7 copy-done.14
  177.6 0.1 reshape.111
  177.7 0.3 copy-done.1
  177.9 5.1 gather_fusion
  183.0 10.7 %all-to-all-start = ((bf16[32,32,512]{2,1,0:T(8,128)(2,1)}), bf16[32,32,512]{2,1,0:T(8,128)(2,1)}, u32[]{:S(2)}, u32[]{:S(2)}) async-start(bf16[32,32,512]{2,1,0:T(8,128)(2,1)} %bitcast.81), calls=%async_computation | async-start | bytes 2097152 | tf_op jit(solution)/shard_map/all_to_all | solution.py:29
  193.7 0.2 all-reduce.3.cloned.1.call-start
  194.0 1.1 convert_element_type.58
  195.1 0.8 copy.42
  195.9 0.1 copy.36
  196.0 0.2 reshape.119
  196.3 0.1 copy.35
  196.4 1.1 reshape.127
  197.5 1.4 fusion.38
  198.9 25.1 %all-to-all-done = bf16[32,32,512]{2,1,0:T(8,128)(2,1)} async-done(((bf16[32,32,512]{2,1,0:T(8,128)(2,1)}), bf16[32,32,512]{2,1,0:T(8,128)(2,1)}, u32[]{:S(2)}, u32[]{:S(2)}) %all-to-all-start) | async-done | bytes 1048608 | tf_op jit(solution)/shard_map/all_to_all | solution.py:29
  224.0 6.0 %fusion.26 = f32[1536,1024]{1,0:T(8,128)} fusion(bf16[512,1024]{1,0:T(8,128)(2,1)} %param.14, bf16[1024,512]{1,0:T(8,128)(2,1)} %bitcast.2, bf16[512,512]{1,0:T(8,128)(2,1)S(1)} %copy-done.1), kind=kOutput, calls=%fused_computation.50 | convolution fusion | flops 1613758464 | bytes 8912896 | tf_op jit(solution)/shard_map/dot_general | solution.py:33
  230.0 25.4 %gather_fusion.1 = f32[4096,1024]{1,0:T(8,128)} fusion(f32[1536,1024]{1,0:T(8,128)} %fusion.26, s32[4096]{0:T(1024)S(1)} %broadcast_clamp_fusion), kind=kCustom, calls=%fused_computation.1 | custom fusion | bytes 33570816 | tf_op jit(solution)/shard_map/gather | solution.py:34
  255.4 19.0 %fusion.34 = (bf16[512,512]{1,0:T(8,128)(2,1)S(1)}, f32[512,8,512]{2,1,0:T(8,128)}, f32[512,8,512]{2,1,0:T(8,128)}, f32[512,512]{1,0:T(8,128)}) fusion(f32[512,8,1024]{2,1,0:T(8,128)} %bitcast.69, f32[512,512]{1,0:T(8,128)} %fusion.38, f32[512,512]{1,0:T(8,128)} %convert_element_type.58, f32[512,8]{1,0:T(8,128)S(1)} %copy.35), kind=kLoop, calls=%fused_computation.65 | loop fusion | flops 28835840 | bytes 37240832 | tf_op jit(solution)/shard_map/reduce_sum | solution.py:106
  274.4 38.4 %scatter_custom_fusion = f32[1536,1024]{1,0:T(8,128)} fusion(s32[4096]{0:T(1024)S(1)} %reshape.127, f32[512,8,512]{2,1,0:T(8,128)} %get-tuple-element.36, f32[]{:T(128)} %constant.2.clone.1, f32[512,8,512]{2,1,0:T(8,128)} %get-tuple-element.35, f32[]{:T(128)} %constant.7.clone.1), kind=kCustom, calls=%fused_computation.10 | custom fusion | flops 8388608 | bytes 23068680 | tf_op jit(solution)/shard_map/scatter-add | solution.py:108
  312.8 1.5 convolution_bitcast_fusion.1
  314.3 6.2 %fusion.20 = f32[512,1024]{1,0:T(8,128)} fusion(f32[1536,1024]{1,0:T(8,128)} %scatter_custom_fusion, bf16[1024,512]{1,0:T(8,128)(2,1)} %bitcast.2, bf16[512,512]{1,0:T(8,128)(2,1)S(1)} %copy-done.1), kind=kOutput, calls=%fused_computation.36 | convolution fusion | flops 1615331328 | bytes 9961472 | tf_op jit(solution)/shard_map/td,tf->df/dot_general | solution.py:111
  320.5 1.5 fusion.41
  322.0 12.4 %convolution_convert_fusion.2 = bf16[8,64,512]{2,1,0:T(8,128)(2,1)} fusion(bf16[2048,8,64]{0,2,1:T(8,128)(2,1)} %bitcast.74, bf16[8,512,2048]{2,1,0:T(8,128)(2,1)} %copy-done.2), kind=kOutput, calls=%fused_computation.47 | convolution fusion | flops 1074003968 | bytes 19398656 | tf_op jit(solution)/shard_map/hij,jhe->ihe/dot_general | solution.py:86
  334.4 1.7 convert.13
  336.1 1.0 copy-done.10
  337.1 3.7 convolution_bitcast_fusion
  340.8 4.9 fusion.22
  345.8 1.7 copy-done.12
  347.4 1.1 slice.64
  348.6 4.9 all-to-all-start.2
  353.5 0.1 reshape.135
  353.6 2.9 fusion.25
  356.5 2.8 fusion.24
  359.3 1.4 convolution_add_fusion
  360.7 12.7 %all-to-all-done.2 = bf16[32,32,512]{2,1,0:T(8,128)(2,1)} async-done(((bf16[32,32,512]{2,1,0:T(8,128)(2,1)}), bf16[32,32,512]{2,1,0:T(8,128)(2,1)}, u32[]{:S(2)}, u32[]{:S(2)}) %all-to-all-start.2) | async-done | bytes 1048608 | tf_op jit(solution)/shard_map/all_to_all | solution.py:114
  373.4 9.4 %scatter_custom_fusion.1 = f32[512,512]{1,0:T(8,128)} fusion(f32[512,512]{1,0:T(8,128)} %convolution_add_fusion, s32[1024]{0:T(1024)S(1)} %reshape.135, bf16[1024,512]{1,0:T(8,128)(2,1)} %bitcast.27), kind=kCustom, calls=%fused_computation.32 | custom fusion | flops 1048576 | bytes 2097152 | tf_op jit(solution)/shard_map/scatter-add | solution.py:121
  382.8 2.1 convert_element_type.66
  384.9 122.4 %all-reduce.3.cloned.1.call-done = (f32[512,512]{0,1:T(8,128)}, f32[512,1024]{1,0:T(8,128)}, f32[512,1536]{0,1:T(8,128)}, f32[512,512]{1,0:T(8,128)}) async-done(((f32[512,512]{0,1:T(8,128)}, f32[512,1024]{1,0:T(8,128)}, f32[512,1536]{0,1:T(8,128)}, f32[512,512]{1,0:T(8,128)}), (f32[512,512]{0,1:T(8,128)}, f32[512,1024]{1,0:T(8,128)}, f32[512,1536]{0,1:T(8,128)}, ...) | async-done | bytes 7340048 | tf_op jit(solution)/shard_map/psum | solution.py:128
  507.3 2.6 copy.43
  509.9 3.5 copy.44
  513.4 3.2 copy.50
  516.6 1.0 copy.51
  (37 shorter events, 0.1 us)
Async XLA Ops:
  7.2 1.4 copy-start
  10.6 1.1 copy-start.6
  14.3 8.7 %slice-start = ((bf16[512,1536]{1,0:T(8,128)(2,1)}), bf16[512,512]{1,0:T(8,128)(2,1)S(1)}, s32[]{:S(2)}) async-start(bf16[512,1536]{1,0:T(8,128)(2,1)} %copy-done.6), calls=%async_computation.6 | async-start | bytes 1048576 | tf_op jit(solution)/shard_map/slice | solution.py:41
  16.7 7.4 %copy-start.3 = (bf16[512,512]{1,0:T(8,128)(2,1)S(1)}, bf16[512,512]{1,0:T(8,128)(2,1)}, u32[]{:S(2)}) copy-start(bf16[512,512]{1,0:T(8,128)(2,1)} %param.17) | copy-start | bytes 1572868
  16.7 7.4 %copy-start.5 = (bf16[512,512]{1,0:T(8,128)(2,1)S(1)}, bf16[512,512]{1,0:T(8,128)(2,1)}, u32[]{:S(2)}) copy-start(bf16[512,512]{1,0:T(8,128)(2,1)} %param.16) | copy-start | bytes 1572868
  16.7 53.8 %all-to-all-start.1 = ((bf16[4,512,1024]{1,2,0:T(8,128)(2,1)}), bf16[4,512,1024]{1,2,0:T(8,128)(2,1)}, u32[]{:S(2)}, u32[]{:S(2)}) async-start(bf16[4,512,1024]{1,2,0:T(8,128)(2,1)} %stack.2), calls=%async_computation.1 | async-start | bytes 8388608 | tf_op jit(solution)/shard_map/all_to_all | solution.py:44
  23.0 311.4 %reduce-scatter.2.cloned.1.call-start = ((), (), s32[]{:S(2)}) async-start(), calls=%async_computation.4 | async-start | bytes 10485760 | tf_op jit(solution)/shard_map/reduce_scatter | solution.py:92
  81.2 7.9 %copy-start.9 = (bf16[512,512]{0,1:T(8,128)(2,1)S(1)}, bf16[512,512]{0,1:T(8,128)(2,1)}, u32[]{:S(2)}) copy-start(bf16[512,512]{0,1:T(8,128)(2,1)} %copy.40) | copy-start | bytes 1572868
  162.1 7.0 %copy-start.2 = (bf16[8,512,2048]{2,1,0:T(8,128)(2,1)}, bf16[8,512,2048]{2,1,0:T(8,128)(2,1)S(1)}, u32[]{:S(2)}) copy-start(bf16[8,512,2048]{2,1,0:T(8,128)(2,1)S(1)} %multiply_convert_fusion) | copy-start | bytes 50331652
  176.9 0.7 copy-start.14
  176.9 1.1 copy-start.1
  177.9 17.1 %copy-start.13 = (s32[512,8]{0,1:T(8,128)S(1)}, s32[512,8]{0,1:T(8,128)}, u32[]{:S(2)}) copy-start(s32[512,8]{0,1:T(8,128)} %param.11) | copy-start | bytes 49156
  177.9 18.3 %copy-start.15 = (s32[512,8]{0,1:T(8,128)S(1)}, s32[512,8]{0,1:T(8,128)}, u32[]{:S(2)}) copy-start(s32[512,8]{0,1:T(8,128)} %param.12) | copy-start | bytes 49156
  177.9 19.6 %copy-start.7 = (bf16[512,512]{1,0:T(8,128)(2,1)S(1)}, bf16[512,512]{1,0:T(8,128)(2,1)}, u32[]{:S(2)}) copy-start(bf16[512,512]{1,0:T(8,128)(2,1)} %param.13) | copy-start | bytes 1572868
  183.0 41.0 %all-to-all-start = ((bf16[32,32,512]{2,1,0:T(8,128)(2,1)}), bf16[32,32,512]{2,1,0:T(8,128)(2,1)}, u32[]{:S(2)}, u32[]{:S(2)}) async-start(bf16[32,32,512]{2,1,0:T(8,128)(2,1)} %bitcast.81), calls=%async_computation | async-start | bytes 2097152 | tf_op jit(solution)/shard_map/all_to_all | solution.py:29
  193.7 313.5 %all-reduce.3.cloned.1.call-start = ((), (), s32[]{:S(2)}) async-start(), calls=%async_computation.5 | async-start | bytes 14680064 | tf_op jit(solution)/shard_map/psum | solution.py:128
  312.8 7.7 %copy-start.4 = (bf16[8,64,512]{2,1,0:T(8,128)(2,1)S(1)}, bf16[8,64,512]{2,1,0:T(8,128)(2,1)}, u32[]{:S(2)}) copy-start(bf16[8,64,512]{2,1,0:T(8,128)(2,1)} %get-tuple-element.43) | copy-start | bytes 1572868
  336.1 1.0 copy-start.10
  345.8 1.7 copy-start.12
  348.6 24.9 %all-to-all-start.2 = ((bf16[32,32,512]{2,1,0:T(8,128)(2,1)}), bf16[32,32,512]{2,1,0:T(8,128)(2,1)}, u32[]{:S(2)}, u32[]{:S(2)}) async-start(bf16[32,32,512]{2,1,0:T(8,128)(2,1)} %bitcast.82), calls=%async_computation.3 | async-start | bytes 2097152 | tf_op jit(solution)/shard_map/all_to_all | solution.py:114
  353.6 5.7 %copy-start.8 = (bf16[512,512]{1,0:T(8,128)(2,1)S(1)}, bf16[512,512]{1,0:T(8,128)(2,1)}, u32[]{:S(2)}) copy-start(bf16[512,512]{1,0:T(8,128)(2,1)} %param.13) | copy-start | bytes 1572868
  507.3 9.3 %copy-start.11 = (f32[512,512]{1,0:T(8,128)S(1)}, f32[512,512]{1,0:T(8,128)}, u32[]{:S(2)}) copy-start(f32[512,512]{1,0:T(8,128)} %get-tuple-element.49) | copy-start | bytes 3145732
Sparse Core Ops, SparseCore 0:
  177.0 93.1 reduce-scatter.1
  341.0 166.2 all-reduce.2
